TPU v7x, 256 devices: a whole 4x4x8 slice. The times are simulated.
256 devices in a mesh: dp: 32 (over x_hi, z, core), fsdp: 8 (over x_lo, y).
Axes of the slice: x: 4 (x_hi: 2, x_lo: 2; x = x_hi * 2 + x_lo), y: 4, z: 8, core: 2. Of those that a mesh axis runs over, the one named last changes fastest.
Arguments:
- states: bfloat16 [49152, 5120], P(('dp', 'fsdp')), may hold values from -24 to 24
- steps: int32 [256], P(('dp', 'fsdp')), may hold values from 0 to 999
- frozen_query_rows: bfloat16 [49152, 5120], P(('dp', 'fsdp')), may hold values from -6 to 6
- frozen_key_rows: bfloat16 [49152, 5120], P(('dp', 'fsdp')), may hold values from -18 to 18
- frozen_value_rows: bfloat16 [49152, 5120], P(('dp', 'fsdp')), may hold values from -6 to 6
- cotangent: bfloat16 [49152, 5120], P(('dp', 'fsdp')), may hold values from -24 to 24
- adapter_down_maps: bfloat16 [2, 5120, 128], P(None, 'fsdp'), may hold values from -0.078125 to 0.078125
- adapter_up_maps: bfloat16 [2, 128, 5120], P(None, None, 'fsdp'), may hold values from -0.5 to 0.5
Outputs:
- grad_down: float32 [2, 5120, 128], P(None, 'fsdp')
- grad_up: float32 [2, 128, 5120], P(None, None, 'fsdp')
All inputs are finite; a program needn't handle non-finite values.
Results may differ from a plain program's by a relative error of at most 0.012.
Values may be sent and summed in bfloat16 or wider, within the bound.
No kernel may reach another device: no remote copies, remote signals or barrier semaphores. Data moves between devices by JAX's collectives and lax.ppermute only.
A program may use at most 128 MiB of HBM per device.

v0:
```python
import math
import jax
import jax.numpy as jnp
from jax import lax
from jax.sharding import PartitionSpec as P

HEADS = 40
NSTEPS = 1000


def rounded(value):
    return lax.optimization_barrier(value.astype(jnp.bfloat16)).astype(jnp.float32)


def clip_objective(
    down_matrix,
    up_matrix,
    states,
    frozen_query_rows,
    frozen_key_rows,
    frozen_value_rows,
    cotangent,
    weight,
):
    highest = lax.Precision.HIGHEST
    length = states.shape[0]
    width = states.shape[1]
    head_size = width // HEADS
    inputs = states.astype(jnp.float32)
    center = inputs - jnp.mean(inputs, axis=1, keepdims=True)
    spread = jnp.mean(center * center, axis=1, keepdims=True)
    normed = rounded(center * lax.rsqrt(spread + 1e-06))
    low = rounded(jnp.einsum("td,jdr->jtr", normed, down_matrix, precision=highest))
    delta = jnp.einsum("jtr,jrd->jtd", low, up_matrix, precision=highest)
    query = rounded(frozen_query_rows.astype(jnp.float32) + delta[0]).reshape(
        length, HEADS, head_size
    )
    value = rounded(frozen_value_rows.astype(jnp.float32) + delta[1]).reshape(
        length, HEADS, head_size
    )
    keys = frozen_key_rows.astype(jnp.float32).reshape(length, HEADS, head_size)
    scores = jnp.einsum("qhe,khe->hqk", query, keys, precision=highest) * (
        1.0 / math.sqrt(head_size)
    )
    probs = rounded(jax.nn.softmax(scores, axis=-1))
    attended = jnp.einsum("hqk,khe->qhe", probs, value, precision=highest).reshape(length, width)
    return weight * jnp.sum(attended * cotangent.astype(jnp.float32))


def local(
    states,
    steps,
    frozen_query_rows,
    frozen_key_rows,
    frozen_value_rows,
    cotangent,
    adapter_down_maps,
    adapter_up_maps,
):
    down_matrix, up_matrix = (
        lax.all_gather(adapter_down_maps, "fsdp", axis=1, tiled=True),
        lax.all_gather(adapter_up_maps, "fsdp", axis=2, tiled=True),
    )
    weight = (steps[0].astype(jnp.float32) + 1.0) / NSTEPS
    grad_fn = jax.grad(clip_objective, argnums=(0, 1))
    local_down, local_up = grad_fn(
        down_matrix.astype(jnp.float32),
        up_matrix.astype(jnp.float32),
        states,
        frozen_query_rows,
        frozen_key_rows,
        frozen_value_rows,
        cotangent,
        weight,
    )
    data_count = lax.axis_size("dp")
    group_count = lax.axis_size("fsdp")
    width = local_down.shape[1]
    rank_size = local_down.shape[2]
    factor = 1.0 / math.sqrt(states.shape[0] * data_count * group_count)
    rows = width // (data_count * group_count)
    pieces_down = (
        local_down.reshape(2, group_count, data_count, rows, rank_size)
        .transpose(2, 1, 0, 3, 4)
        .reshape(data_count * group_count, 2, rows, rank_size)
    )
    pieces_up = (
        local_up.reshape(2, rank_size, group_count, data_count, rows)
        .transpose(3, 2, 0, 1, 4)
        .reshape(data_count * group_count, 2, rank_size, rows)
    )
    summed_down, summed_up = (
        lax.psum_scatter(pieces_down, ("dp", "fsdp"), scatter_dimension=0, tiled=True),
        lax.psum_scatter(pieces_up, ("dp", "fsdp"), scatter_dimension=0, tiled=True),
    )
    joined_down, joined_up = (
        lax.all_gather(summed_down, "dp", axis=0, tiled=True),
        lax.all_gather(summed_up, "dp", axis=0, tiled=True),
    )
    shard_down = joined_down.transpose(1, 0, 2, 3).reshape(2, data_count * rows, rank_size)
    shard_up = joined_up.transpose(1, 2, 0, 3).reshape(2, rank_size, data_count * rows)
    return (shard_down * factor, shard_up * factor)


def solution(mesh):
    in_specs = (
        P(("dp", "fsdp"), None),
        P(("dp", "fsdp")),
        P(("dp", "fsdp"), None),
        P(("dp", "fsdp"), None),
        P(("dp", "fsdp"), None),
        P(("dp", "fsdp"), None),
        P(None, "fsdp", None),
        P(None, None, "fsdp"),
    )
    out_specs = (P(None, "fsdp", None), P(None, None, "fsdp"))
    return jax.shard_map(local, mesh=mesh, in_specs=in_specs, out_specs=out_specs, check_vma=False)
```

profile of v0, /device:TPU:1, one launch (start us, length us, event | category | flops | bytes accessed | tf_op | source)
XLA Modules:
  0.0 570.8 jit_solution(748312822632556784)
XLA Ops:
  7.2 0.0 copy-start
  7.2 0.0 all-gather.3.cloned.1.call-start
  7.2 0.7 all-gather.3.cloned.1.call-update
  7.9 0.0 all-gather.5.cloned.1.call-start
  8.0 0.7 all-gather.5.cloned.1.call-update
  8.7 0.0 all-reduce.7.cloned.1.call-start
  8.7 0.0 copy-start.2
  8.7 2.0 convert_reduce_fusion
  10.8 2.2 fusion.19
  13.0 0.0 copy-done.2
  13.0 1.9 fusion.20
  15.6 39.7 %all-gather.3.cloned.1.call-done = bf16[2,5120,128]{2,1,0:T(8,128)(2,1)} async-done(((bf16[2,640,128]{2,1,0:T(8,128)(2,1)}), bf16[2,5120,128]{2,1,0:T(8,128)(2,1)}) %all-gather.3.cloned.1.call-update) | async-done | bytes 2621456 | tf_op jit(solution)/shard_map/all_gather | solution.py:61
  55.2 3.0 fusion.54
  58.3 43.5 %all-gather.5.cloned.1.call-done = bf16[2,128,5120]{2,1,0:T(8,128)(2,1)} async-done(((bf16[2,128,640]{2,1,0:T(8,128)(2,1)}), bf16[2,128,5120]{2,1,0:T(8,128)(2,1)}) %all-gather.5.cloned.1.call-update) | async-done | bytes 2621456 | tf_op jit(solution)/shard_map/all_gather | solution.py:62
  101.8 0.0 copy-start.10
  101.8 0.0 copy-start.11
  101.8 3.1 fusion.63
  104.9 0.0 copy-done.10
  104.9 0.0 copy-done.11
  104.9 1.2 fusion.24
  106.1 0.0 copy-done
  106.1 1.2 fusion.37
  107.3 0.0 copy-start.7
  107.3 6.3 %fusion.62 = (f32[40,192]{1,0:T(8,128)S(1)}, f32[40,192,192]{1,2,0:T(8,128)S(1)}) fusion(f32[40,192,192]{1,2,0:T(8,128)S(1)} %fusion.37), kind=kOutput, calls=%fused_computation.77 | output fusion | flops 5898431 | bytes 11827200 | tf_op jit(solution)/shard_map/jvp()/sub | solution.py:45
  113.7 0.0 copy-done.7
  113.7 3.6 fusion.33
  117.3 0.0 copy-start.3
  117.3 2.9 divide_convert_fusion
  120.2 0.0 copy-done.3
  120.2 11.1 %convert_bitcast_fusion = bf16[40,24,8,128]{3,2,1,0:T(8,128)(2,1)} fusion(f32[40,192,192]{1,2,0:T(8,128)S(1)} %get-tuple-element.13, bf16[40,192,192]{1,2,0:T(8,128)(2,1)} %copy-done.3, f32[40,192]{1,0:T(8,128)S(1)} %neg.6, f32[40,192]{1,0:T(8,128)S(1)} %get-tuple-element.12, bf16[192,5120]{1,0:T(8,128)(2,1)S(1)} %copy-done), kind=kOutput, calls=%fused_computation.58 | convolution fusion | flops 2273280000 | bytes 12840960 | tf_op jit(solution)/shard_map/transpose(jvp(qhe,khe->hqk))/dot_general | solution.py:42
  131.3 0.0 copy-start.8
  131.3 2.2 copy.93
  133.5 0.0 copy-done.8
  133.5 3.6 convert_bitcast_fusion.1
  137.1 0.9 copy.94
  138.0 0.0 copy-start.4
  138.0 1.3 copy-done.4
  139.3 5.6 fusion.8
  144.9 8.7 %copy.46 = f32[2,128,5120]{1,0,2:T(2,128)} copy(f32[2,128,5120]{2,1,0:T(8,128)} %fusion.8) | data formatting | bytes 10485760 | tf_op jit(solution)/shard_map/transpose(jvp(jtr,jrd->jtd))/dot_general | solution.py:34
  153.6 5.5 copy.91
  159.1 0.0 copy-start.5
  159.1 0.0 copy-start.9
  159.2 6.3 %copy.48 = f32[256,2,128,20]{2,1,3,0:T(2,128)} copy(f32[256,2,128,20]{2,0,3,1:T(8,128)S(1)} %bitcast.118) | data formatting | bytes 10485760 | tf_op jit(solution)/shard_map/reshape | solution.py:90
  165.5 0.0 copy-done.5
  165.5 0.0 copy-done.9
  165.5 0.0 copy-start.6
  165.5 3.6 fusion.53
  169.1 0.0 copy-done.6
  169.1 3.2 convolution_bitcast_fusion
  172.3 8.8 %copy.43 = f32[2,5120,128]{2,0,1:T(2,128)} copy(f32[2,5120,128]{1,2,0:T(8,128)} %convolution_bitcast_fusion) | data formatting | bytes 10485760 | tf_op jit(solution)/shard_map/transpose(jvp(td,jdr->jtr))/transpose | solution.py:33
  181.2 5.5 copy.92
  186.7 6.3 %copy.45 = f32[256,2,20,128]{3,1,2,0:T(2,128)} copy(f32[256,2,20,128]{3,0,2,1:T(8,128)S(1)} %bitcast.120) | data formatting | bytes 10485760 | tf_op jit(solution)/shard_map/reshape | solution.py:85
  193.0 0.0 all-reduce.7.cloned.1.call-update
  193.0 0.0 copy-start.1
  193.0 285.5 %all-reduce.7.cloned.1.call-done = (f32[256,2,20,128]{3,1,2,0:T(2,128)}, f32[256,2,128,20]{2,1,3,0:T(2,128)}) async-done(((f32[256,2,20,128]{3,1,2,0:T(2,128)}, f32[256,2,128,20]{2,1,3,0:T(2,128)}), (f32[256,2,20,128]{3,1,2,0:T(2,128)}, f32[256,2,128,20]{2,1,3,0:T(2,128)})) %all-reduce.7.cloned.1.call-update) | async-done | bytes 10485776
  478.5 0.7 constant_dynamic-slice_fusion.1
  479.2 42.7 %all_gather.14 = f32[32,2,20,128]{3,1,2,0:T(2,128)S(1)} all-gather(f32[1,2,20,128]{3,1,2,0:T(2,128)S(1)} %constant_dynamic-slice_fusion.1), channel_id=1, replica_groups=mesh['dp'=32,'fsdp'=8] {'dp'}, dimensions={0}, use_global_device_ids=true | all-gather | bytes 675840 | tf_op jit(solution)/shard_map/all_gather | solution.py:97
  521.9 0.3 broadcast_multiply_fusion.1
  522.3 0.9 copy.49
  523.1 0.7 constant_dynamic-slice_fusion
  523.9 38.5 %all_gather.15 = f32[32,2,128,20]{2,1,3,0:T(2,128)S(1)} all-gather(f32[1,2,128,20]{2,1,3,0:T(2,128)S(1)} %constant_dynamic-slice_fusion), channel_id=1, replica_groups=mesh['dp'=32,'fsdp'=8] {'dp'}, dimensions={0}, use_global_device_ids=true | all-gather | bytes 675840 | tf_op jit(solution)/shard_map/all_gather | solution.py:98
  562.3 0.3 broadcast_multiply_fusion
  562.7 1.4 copy.50
  564.1 0.0 copy-done.1
  (4 shorter events, 0.0 us)
Async XLA Ops:
  7.2 98.9 %copy-start = (bf16[192,5120]{1,0:T(8,128)(2,1)S(1)}, bf16[192,5120]{1,0:T(8,128)(2,1)}, u32[]{:S(2)}) copy-start(bf16[192,5120]{1,0:T(8,128)(2,1)} %param.11) | copy-start | bytes 5898244
  7.2 48.1 %all-gather.3.cloned.1.call-start = ((), (), s32[]{:S(2)}) async-start(), calls=%async_computation | async-start | bytes 2949120 | tf_op jit(solution)/shard_map/all_gather | solution.py:61
  7.9 93.9 %all-gather.5.cloned.1.call-start = ((), (), s32[]{:S(2)}) async-start(), calls=%async_computation.1 | async-start | bytes 2949120 | tf_op jit(solution)/shard_map/all_gather | solution.py:62
  8.7 469.9 %all-reduce.7.cloned.1.call-start = ((), (), s32[]{:S(2)}) async-start(), calls=%async_computation.2 | async-start | bytes 20971520
  8.7 4.3 copy-start.2
  101.8 3.1 copy-start.10
  101.8 3.1 copy-start.11
  107.3 6.3 %copy-start.7 = (bf16[192,5120]{1,0:T(8,128)(2,1)S(1)}, bf16[192,5120]{1,0:T(8,128)(2,1)}, u32[]{:S(2)}) copy-start(bf16[192,5120]{1,0:T(8,128)(2,1)} %param.13) | copy-start | bytes 5898244
  117.3 2.9 copy-start.3
  131.3 2.2 copy-start.8
  138.0 1.3 copy-start.4
  159.1 6.4 %copy-start.5 = (bf16[40,24,8,128]{3,2,0,1:T(8,128)(2,1)S(1)}, bf16[40,24,8,128]{3,2,0,1:T(8,128)(2,1)}, u32[]{:S(2)}) copy-start(bf16[40,24,8,128]{3,2,0,1:T(8,128)(2,1)} %copy-done.4) | copy-start | bytes 5898244
  159.1 6.4 %copy-start.9 = (bf16[2,128,5120]{2,1,0:T(8,128)(2,1)S(1)}, bf16[2,128,5120]{2,1,0:T(8,128)(2,1)}, u32[]{:S(2)}) copy-start(bf16[2,128,5120]{2,1,0:T(8,128)(2,1)} %all-gather.5.cloned.1.call-done) | copy-start | bytes 7864324
  165.5 3.6 copy-start.6
  193.0 371.0 %copy-start.1 = (bf16[192,5120]{1,0:T(8,128)(2,1)S(1)}, bf16[192,5120]{1,0:T(8,128)(2,1)}, u32[]{:S(2)}) copy-start(bf16[192,5120]{1,0:T(8,128)(2,1)} %param.11) | copy-start | bytes 5898244
Sparse Core Ops, SparseCore 0:
  9.8 45.3 all-gather.2
  57.0 44.7 all-gather.4
  193.1 285.3 all-reduce.6
where the time goes:
time: 578 us; the launch traced here: 571 us
  waiting for transfers between devices  370 us (64%)
  blocking collectives  81.1 us (14%)
  local copies, waits for them, and re-layouts  49.4 us (9%)
  matrix products  37.9 us (7%)
  other arithmetic  17.3 us (3%)
  between operations  14.8 us (3%)
    unnamed x4, waiting for transfers between devices  287 us
    all_gather x1, waiting for transfers between devices, local(): lax.all_gather(adapter_up_maps, 'fsdp', axis=2, tiled=True)  43.5 us
    all_gather x1, blocking collectives, local(): lax.all_gather(summed_down, 'dp', axis=0, tiled=True)  42.7 us
    all_gather x1, waiting for transfers between devices, local(): lax.all_gather(adapter_down_maps, 'fsdp', axis=1, tiled=True)  39.7 us
    all_gather x1, blocking collectives, local(): lax.all_gather(summed_up, 'dp', axis=0, tiled=True)  38.5 us
    dot_general x3, matrix products, clip_objective(): delta = jnp.einsum('jtr,jrd->jtd', low, up_matrix, precision=highest)  12.3 us
    dot_general x2, matrix products, clip_objective(): jnp.einsum('qhe,khe->hqk', query, keys, precision=highest)  12.3 us
  transfers between devices with their start and end apart: 3, of which 3 were waited for; matrix products, arithmetic and copies ran while one was open for 2% of the time, Pallas kernels for 0%

commit v1 on v0

--- a/solution.py
+++ b/solution.py
@@ -3,6 +3,7 @@
 import jax.numpy as jnp
 from jax import lax
 from jax.sharding import PartitionSpec as P
+from jax.lax import all_to_all, axis_size
 
 HEADS = 40
 NSTEPS = 1000
@@ -93,8 +94,11 @@
         lax.psum_scatter(pieces_down, ("dp", "fsdp"), scatter_dimension=0, tiled=True),
         lax.psum_scatter(pieces_up, ("dp", "fsdp"), scatter_dimension=0, tiled=True),
     )
+    place_node = lambda frame, array_dim: jnp.concatenate(
+        all_to_all(jnp.stack([frame] * axis_size("dp"), axis=0), "dp", 0, 0), array_dim
+    )
     joined_down, joined_up = (
-        lax.all_gather(summed_down, "dp", axis=0, tiled=True),
+        place_node(summed_down, 0),
         lax.all_gather(summed_up, "dp", axis=0, tiled=True),
     )
     shard_down = joined_down.transpose(1, 0, 2, 3).reshape(2, data_count * rows, rank_size)

time: 578 us -> 561 us (0.971)
  blocking collectives: 81.1 us -> 51.7 us
  starting transfers between devices: 0.11 us -> 11 us
    all_gather x1 -> x0, blocking collectives: 42.7 us -> none  [local(): lax.all_gather(summed_down, 'dp', axis=0, tiled=True)]
    all_gather x1, blocking collectives: 38.5 us -> 51.7 us  [local(): lax.all_gather(summed_up, 'dp', axis=0, tiled=True)]
    all_to_all x0 -> x1, starting transfers between devices: none -> 10.9 us  [local(): all_to_all(jnp.stack([frame] * axis_size('dp'), axis=0), 'dp', 0, 0)]
  transfers between devices with their start and end apart: 3 -> 4, of which waited for: 3 -> 3; matrix products, arithmetic and copies ran while one was open for 2% -> 2% of each run, Pallas kernels for 0% -> 0%
where the time goes in v1:
time: 561 us; the launch traced here: 554 us
  waiting for transfers between devices  370 us (66%)
  blocking collectives  51.7 us (9%)
  local copies, waits for them, and re-layouts  50.6 us (9%)
  matrix products  37.9 us (7%)
  other arithmetic  17.3 us (3%)
  between operations  14.8 us (3%)
  starting transfers between devices  11 us (2%)
    unnamed x4, waiting for transfers between devices  287 us
    all_gather x1, blocking collectives, local(): lax.all_gather(summed_up, 'dp', axis=0, tiled=True)  51.7 us
    all_gather x1, waiting for transfers between devices, local(): lax.all_gather(adapter_up_maps, 'fsdp', axis=2, tiled=True)  43.5 us
    all_gather x1, waiting for transfers between devices, local(): lax.all_gather(adapter_down_maps, 'fsdp', axis=1, tiled=True)  39.7 us
    dot_general x2, matrix products, clip_objective(): jnp.einsum('qhe,khe->hqk', query, keys, precision=highest)  12.3 us
    dot_general x3, matrix products, clip_objective(): delta = jnp.einsum('jtr,jrd->jtd', low, up_matrix, precision=highest)  12.3 us
  transfers between devices with their start and end apart: 4, of which 3 were waited for; matrix products, arithmetic and copies ran while one was open for 2% of the time, Pallas kernels for 0%

profile of v1, /device:TPU:1, one launch (start us, length us, event | category | flops | bytes accessed | tf_op | source)
XLA Modules:
  0.0 553.5 jit_solution(2721909570493853553)
XLA Ops:
  7.2 0.0 copy-start
  7.2 0.0 all-gather.3.cloned.1.call-start
  7.2 0.7 all-gather.3.cloned.1.call-update
  7.9 0.0 all-gather.5.cloned.1.call-start
  8.0 0.7 all-gather.5.cloned.1.call-update
  8.7 0.0 all-reduce.7.cloned.1.call-start
  8.7 0.0 copy-start.2
  8.7 2.0 convert_reduce_fusion
  10.8 2.2 fusion.19
  13.0 0.0 copy-done.2
  13.0 1.9 fusion.20
  15.6 39.7 %all-gather.3.cloned.1.call-done = bf16[2,5120,128]{2,1,0:T(8,128)(2,1)} async-done(((bf16[2,640,128]{2,1,0:T(8,128)(2,1)}), bf16[2,5120,128]{2,1,0:T(8,128)(2,1)}) %all-gather.3.cloned.1.call-update) | async-done | bytes 2621456 | tf_op jit(solution)/shard_map/all_gather | solution.py:62
  55.2 3.0 fusion.54
  58.3 43.5 %all-gather.5.cloned.1.call-done = bf16[2,128,5120]{2,1,0:T(8,128)(2,1)} async-done(((bf16[2,128,640]{2,1,0:T(8,128)(2,1)}), bf16[2,128,5120]{2,1,0:T(8,128)(2,1)}) %all-gather.5.cloned.1.call-update) | async-done | bytes 2621456 | tf_op jit(solution)/shard_map/all_gather | solution.py:63
  101.8 0.0 copy-start.11
  101.8 3.1 fusion.63
  104.9 0.0 copy-done.10
  104.9 0.0 copy-done.11
  104.9 1.2 fusion.24
  106.1 0.0 copy-done
  106.1 1.2 fusion.37
  107.3 0.0 copy-start.7
  107.3 6.3 %fusion.62 = (f32[40,192]{1,0:T(8,128)S(1)}, f32[40,192,192]{1,2,0:T(8,128)S(1)}) fusion(f32[40,192,192]{1,2,0:T(8,128)S(1)} %fusion.37), kind=kOutput, calls=%fused_computation.77 | output fusion | flops 5898431 | bytes 11827200 | tf_op jit(solution)/shard_map/jvp()/sub | solution.py:46
  113.7 0.0 copy-done.7
  113.7 3.6 fusion.33
  117.3 0.0 copy-start.3
  117.3 2.9 divide_convert_fusion
  120.2 0.0 copy-done.3
  120.2 11.1 %convert_bitcast_fusion = bf16[40,24,8,128]{3,2,1,0:T(8,128)(2,1)} fusion(f32[40,192,192]{1,2,0:T(8,128)S(1)} %get-tuple-element.15, bf16[40,192,192]{1,2,0:T(8,128)(2,1)} %copy-done.3, f32[40,192]{1,0:T(8,128)S(1)} %neg.6, f32[40,192]{1,0:T(8,128)S(1)} %get-tuple-element.14, bf16[192,5120]{1,0:T(8,128)(2,1)S(1)} %copy-done), kind=kOutput, calls=%fused_computation.58 | convolution fusion | flops 2273280000 | bytes 12840960 | tf_op jit(solution)/shard_map/transpose(jvp(qhe,khe->hqk))/dot_general | solution.py:43
  131.3 0.0 copy-start.8
  131.3 2.2 copy.110
  133.5 0.0 copy-done.8
  133.5 3.6 convert_bitcast_fusion.1
  137.1 0.9 copy.111
  138.0 0.0 copy-start.4
  138.0 1.3 copy-done.4
  139.3 5.6 %fusion.8 = f32[2,128,5120]{2,1,0:T(8,128)} fusion(bf16[2,192,128]{2,1,0:T(8,128)(2,1)S(1)} %fusion.54, bf16[1,192,5120]{2,1,0:T(8,128)(2,1)S(1)} %bitcast.125, bf16[1,192,5120]{2,1,0:T(8,128)(2,1)S(1)} %bitcast.127), kind=kOutput, calls=%fused_computation.12 | convolution fusion | flops 3025797120 | bytes 9273344 | tf_op jit(solution)/shard_map/transpose(jvp(jtr,jrd->jtd))/dot_general | solution.py:35
  144.9 8.7 %copy.63 = f32[2,128,5120]{1,0,2:T(2,128)} copy(f32[2,128,5120]{2,1,0:T(8,128)} %fusion.8) | data formatting | bytes 10485760 | tf_op jit(solution)/shard_map/transpose(jvp(jtr,jrd->jtd))/dot_general | solution.py:35
  153.6 5.5 copy.108
  159.1 0.0 copy-start.5
  159.2 0.0 copy-start.9
  159.2 6.3 %copy.65 = f32[256,2,128,20]{2,1,3,0:T(2,128)} copy(f32[256,2,128,20]{2,0,3,1:T(8,128)S(1)} %bitcast.122) | data formatting | bytes 10485760 | tf_op jit(solution)/shard_map/reshape | solution.py:91
  165.5 0.0 copy-done.5
  165.5 0.0 copy-done.9
  165.5 0.0 copy-start.6
  165.5 3.6 fusion.53
  169.1 0.0 copy-done.6
  169.1 3.2 convolution_bitcast_fusion
  172.3 8.8 %copy.60 = f32[2,5120,128]{2,0,1:T(2,128)} copy(f32[2,5120,128]{1,2,0:T(8,128)} %convolution_bitcast_fusion) | data formatting | bytes 10485760 | tf_op jit(solution)/shard_map/transpose(jvp(td,jdr->jtr))/transpose | solution.py:34
  181.2 5.5 copy.109
  186.7 6.3 %copy.62 = f32[256,2,20,128]{3,1,2,0:T(2,128)} copy(f32[256,2,20,128]{3,0,2,1:T(8,128)S(1)} %bitcast.124) | data formatting | bytes 10485760 | tf_op jit(solution)/shard_map/reshape | solution.py:86
  193.0 0.0 all-reduce.7.cloned.1.call-update
  193.0 285.7 %all-reduce.7.cloned.1.call-done = (f32[256,2,20,128]{3,1,2,0:T(2,128)}, f32[256,2,128,20]{2,1,3,0:T(2,128)}) async-done(((f32[256,2,20,128]{3,1,2,0:T(2,128)}, f32[256,2,128,20]{2,1,3,0:T(2,128)}), (f32[256,2,20,128]{3,1,2,0:T(2,128)}, f32[256,2,128,20]{2,1,3,0:T(2,128)})) %all-reduce.7.cloned.1.call-update) | async-done | bytes 10485776
  478.7 0.9 dynamic-slice_bitcast_fusion
  479.6 1.0 stack.2
  480.6 10.9 %all-to-all-start = ((f32[32,1,2,20,128]{4,2,3,1,0:T(2,128)}), f32[32,1,2,20,128]{4,2,3,1,0:T(2,128)S(1)}, u32[]{:S(2)}, u32[]{:S(2)}) async-start(f32[32,1,2,20,128]{4,2,3,1,0:T(2,128)} %stack.2), calls=%async_computation | async-start | bytes 1310720 | tf_op jit(solution)/shard_map/all_to_all | solution.py:98
  491.4 0.7 constant_dynamic-slice_fusion
  492.2 51.7 %all_gather.11 = f32[32,2,128,20]{2,1,3,0:T(2,128)S(1)} all-gather(f32[1,2,128,20]{2,1,3,0:T(2,128)S(1)} %constant_dynamic-slice_fusion), channel_id=1, replica_groups=mesh['dp'=32,'fsdp'=8] {'dp'}, dimensions={0}, use_global_device_ids=true | all-gather | bytes 675840 | tf_op jit(solution)/shard_map/all_gather | solution.py:102
  543.9 0.3 broadcast_multiply_fusion
  544.2 1.4 copy.67
  545.6 0.0 all-to-all-done
  545.6 0.3 broadcast_multiply_fusion.1
  545.9 0.9 copy.66
  546.8 0.0 copy-done.1
  (6 shorter events, 0.0 us)
Async XLA Ops:
  7.2 98.9 %copy-start = (bf16[192,5120]{1,0:T(8,128)(2,1)S(1)}, bf16[192,5120]{1,0:T(8,128)(2,1)}, u32[]{:S(2)}) copy-start(bf16[192,5120]{1,0:T(8,128)(2,1)} %param.11) | copy-start | bytes 5898244
  7.2 48.1 %all-gather.3.cloned.1.call-start = ((), (), s32[]{:S(2)}) async-start(), calls=%async_computation.1 | async-start | bytes 2949120 | tf_op jit(solution)/shard_map/all_gather | solution.py:62
  7.9 93.9 %all-gather.5.cloned.1.call-start = ((), (), s32[]{:S(2)}) async-start(), calls=%async_computation.2 | async-start | bytes 2949120 | tf_op jit(solution)/shard_map/all_gather | solution.py:63
  8.7 470.0 %all-reduce.7.cloned.1.call-start = ((), (), s32[]{:S(2)}) async-start(), calls=%async_computation.3 | async-start | bytes 20971520
  8.7 4.3 copy-start.2
  101.8 3.1 copy-start.10
  101.8 3.1 copy-start.11
  107.3 6.3 %copy-start.7 = (bf16[192,5120]{1,0:T(8,128)(2,1)S(1)}, bf16[192,5120]{1,0:T(8,128)(2,1)}, u32[]{:S(2)}) copy-start(bf16[192,5120]{1,0:T(8,128)(2,1)} %param.13) | copy-start | bytes 5898244
  117.3 2.9 copy-start.3
  131.3 2.2 copy-start.8
  138.0 1.3 copy-start.4
  159.1 6.4 %copy-start.5 = (bf16[40,24,8,128]{3,2,0,1:T(8,128)(2,1)S(1)}, bf16[40,24,8,128]{3,2,0,1:T(8,128)(2,1)}, u32[]{:S(2)}) copy-start(bf16[40,24,8,128]{3,2,0,1:T(8,128)(2,1)} %copy-done.4) | copy-start | bytes 5898244
  159.2 6.4 %copy-start.9 = (bf16[2,128,5120]{2,1,0:T(8,128)(2,1)S(1)}, bf16[2,128,5120]{2,1,0:T(8,128)(2,1)}, u32[]{:S(2)}) copy-start(bf16[2,128,5120]{2,1,0:T(8,128)(2,1)} %all-gather.5.cloned.1.call-done) | copy-start | bytes 7864324
  165.5 3.6 copy-start.6
  478.7 68.1 %copy-start.1 = (bf16[192,5120]{1,0:T(8,128)(2,1)S(1)}, bf16[192,5120]{1,0:T(8,128)(2,1)}, u32[]{:S(2)}) copy-start(bf16[192,5120]{1,0:T(8,128)(2,1)} %param.11) | copy-start | bytes 5898244
  480.6 65.0 %all-to-all-start = ((f32[32,1,2,20,128]{4,2,3,1,0:T(2,128)}), f32[32,1,2,20,128]{4,2,3,1,0:T(2,128)S(1)}, u32[]{:S(2)}, u32[]{:S(2)}) async-start(f32[32,1,2,20,128]{4,2,3,1,0:T(2,128)} %stack.2), calls=%async_computation | async-start | bytes 1310720 | tf_op jit(solution)/shard_map/all_to_all | solution.py:98
Sparse Core Ops, SparseCore 0:
  9.8 45.3 all-gather.2
  57.0 44.7 all-gather.4
  193.1 285.5 all-reduce.6
